TPU v7x, 32 devices: a whole 2x2x4 slice. The times are simulated.
32 devices in a mesh: grp: 2 (over x), row: 16 (over z, y, core).
Axes of the slice: x: 2, y: 2, z: 4, core: 2. Of those that a mesh axis runs over, the one named last changes fastest.
Arguments:
- amps: float32 [1024, 4096], P(('grp', 'row')), parts along dimension 0, may hold values from -6 to 6
- amp_mask: int32 [256, 16], P('grp'), parts along dimension 0, may hold values 0 or 1
- integrals: float32 [256, 256, 256], P(('grp', 'row')), parts along dimension 0, may hold values from -0.09375 to 0.09375
- slot_tile: int32 [256], P('grp'), parts along dimension 0, may hold values from 0 to 127, each once
- int_mask: int32 [256], P('grp'), parts along dimension 0, may hold values 0 or 1
Outputs:
- ladder: float32 [1024, 2048], P(('grp', 'row')), parts along dimension 0
There are 2 independent parts, one for each index of `grp`. A program takes and returns all parts, laid end to end along the dimension named above; each array names one. Nothing has to cross between parts.
All inputs are finite; a program needn't handle non-finite values.
Results may differ from a plain program's by a relative error of at most 0.000071.
Values sent between devices are 32-bit elements; how exact they have to be, the bound alone decides.
A program may use at most 64 MiB of HBM per device.

v0:
```python
import jax
import jax.numpy as jnp
from jax import lax
from jax.sharding import PartitionSpec as P

NV = 2048
TILE = 256
PANELS = 2
PTILE = 4
NT = 8


def local(amps, amp_mask, integrals, slot_tile, int_mask):
    members = lax.axis_size("row")
    position = lax.axis_index("row")
    local_rows = amps.shape[0]
    slot_count = integrals.shape[0]
    column_blocks = PANELS * NT
    mask_rows = lax.dynamic_slice_in_dim(
        amp_mask, position * (local_rows // PTILE), local_rows // PTILE, 0
    )
    mask_full = jnp.repeat(mask_rows.astype(jnp.float32), PTILE, axis=0)
    masked = amps.reshape(local_rows, column_blocks, TILE) * mask_full[:, :, None]
    wanted = (slot_tile // NT).reshape(members, slot_count).T.reshape(-1)
    picked = jnp.take(masked, wanted, axis=1)
    sending = picked.reshape(local_rows, slot_count, members * TILE)
    columns = lax.all_to_all(sending, "row", split_axis=2, concat_axis=0, tiled=True)
    own_tiles = lax.dynamic_slice_in_dim(slot_tile, position * slot_count, slot_count, 0)
    tile_ids = jnp.arange(slot_tile.shape[0], dtype=jnp.int32)
    tile_on = jnp.sum(
        jnp.where(own_tiles[:, None] == tile_ids[None, :], int_mask[None, :], 0), axis=1
    )
    weights = integrals * tile_on.astype(jnp.float32)[:, None, None]
    tile_cols = jnp.arange(NT, dtype=jnp.int32)
    selector = ((own_tiles % NT)[:, None] == tile_cols[None, :]).astype(jnp.float32)
    product = jnp.einsum(
        "psc,sca->psa",
        columns,
        weights,
        precision=lax.Precision.HIGHEST,
        preferred_element_type=jnp.float32,
    )
    spread = jnp.einsum(
        "psa,sb->pba",
        product,
        selector,
        precision=lax.Precision.HIGHEST,
        preferred_element_type=jnp.float32,
    )
    return lax.psum_scatter(
        spread.reshape(local_rows * lax.axis_size("row"), NV),
        "row",
        scatter_dimension=0,
        tiled=True,
    )


def solution(mesh):
    return jax.shard_map(
        local,
        mesh=mesh,
        in_specs=(
            P(("grp", "row"), None),
            P("grp", None),
            P(("grp", "row"), None, None),
            P("grp"),
            P("grp"),
        ),
        out_specs=P(("grp", "row"), None),
        check_vma=False,
    )
```

profile of v0, /device:TPU:0, one launch (start us, length us, event | category | flops | bytes accessed | tf_op | source)
XLA Modules:
  0.0 303.0 jit_solution(4884710751910437067)
XLA Ops:
  6.5 0.0 copy-start
  6.5 0.7 copy-done
  7.2 0.1 constant_dynamic-slice_fusion
  7.3 0.1 copy.67
  7.4 0.1 copy.53
  7.5 0.7 and_select_fusion
  8.1 0.1 reshape.58
  8.2 0.1 copy.55
  8.3 0.1 reshape.60
  8.4 1.2 bitcast_multiply_fusion
  9.6 2.8 gather_fusion
  12.4 6.5 %copy.56 = f32[32,128,256]{2,1,0:T(8,128)} copy(f32[32,128,256]{2,0,1:T(8,128)} %bitcast.32) | data formatting | bytes 8388608 | tf_op jit(solution)/shard_map/jit(_take)/gather | solution.py:25
  18.9 4.9 %gather.7 = f32[32,8,4096]{2,1,0:T(8,128)} reshape(f32[32,128,256]{2,1,0:T(8,128)} %copy.56) | data formatting | bytes 8388608 | tf_op jit(solution)/shard_map/jit(_take)/gather | solution.py:25
  23.9 0.1 broadcast_in_dim.37
  23.9 4.6 %broadcast_select_fusion = f32[32,8,4096]{2,1,0:T(8,128)} fusion(f32[32,8,4096]{2,1,0:T(8,128)} %gather.7, pred[8,4096]{1,0:T(8,128)(4,1)S(1)} %bitcast.35), kind=kLoop, calls=%fused_computation.2 | loop fusion | flops 1048576 | bytes 8421376 | tf_op jit(solution)/shard_map/jit(_take)/select_n | solution.py:25
  28.6 10.8 %copy.57 = f32[32,8,4096]{0,1,2:T(8,128)} copy(f32[32,8,4096]{2,1,0:T(8,128)} %broadcast_select_fusion) | data formatting | bytes 8388608 | tf_op jit(solution)/shard_map/jit(_take)/select_n | solution.py:25
  39.4 16.0 %reshape.71 = f32[16,1,65536]{2,1,0:T(1,128)} reshape(f32[4096,8,32]{2,1,0:T(8,128)} %bitcast.28) | data formatting | bytes 8388608
  55.4 0.0 copy-start.3
  55.4 0.0 copy-start.4
  55.4 7.6 %all-to-all-start = ((f32[16,1,65536]{2,1,0:T(1,128)}), f32[16,1,65536]{2,1,0:T(1,128)}, u32[]{:S(2)}, u32[]{:S(2)}) async-start(f32[16,1,65536]{2,1,0:T(1,128)} %reshape.71), calls=%async_computation | async-start | bytes 8388608 | tf_op jit(solution)/shard_map/all_to_all | solution.py:27
  62.9 0.2 reduce-scatter.2.cloned.1.call-start
  63.2 0.0 copy-done.3
  63.2 0.1 and_select_fusion.1
  63.3 0.0 copy-done.4
  63.3 0.2 select_reduce_fusion
  63.5 77.2 %all-to-all-done = f32[16,1,65536]{2,1,0:T(1,128)} async-done(((f32[16,1,65536]{2,1,0:T(1,128)}), f32[16,1,65536]{2,1,0:T(1,128)}, u32[]{:S(2)}, u32[]{:S(2)}) %all-to-all-start) | async-done | bytes 4194336 | tf_op jit(solution)/shard_map/all_to_all | solution.py:27
  140.6 0.5 broadcast.61
  141.1 14.1 %reduce = f32[16,65536]{1,0:T(8,128)} reduce(f32[16,1,65536]{2,1,0:T(1,128)} %all-to-all-done, f32[]{:T(128)} %broadcast.61), dimensions={1}, to_apply=%all_to_all.13.reduce_sub_computation | reduce | bytes 8388612 | tf_op jit(solution)/shard_map/all_to_all | solution.py:27
  155.3 15.1 %reshape.72 = f32[4096,8,32]{2,1,0:T(8,128)} reshape(f32[16,65536]{1,0:T(8,128)} %reduce) | data formatting | bytes 8388608
  170.4 0.0 copy-start.2
  170.4 11.6 %copy.66 = f32[16,32,8,256]{3,1,0,2:T(8,128)} copy(f32[16,32,8,256]{1,2,3,0:T(8,128)} %bitcast.29) | data formatting | bytes 8388608 | tf_op jit(solution)/shard_map/all_to_all | solution.py:27
  182.0 0.0 copy-done.2
  182.0 12.9 %convolution_bitcast_fusion = f32[512,8,256]{0,2,1:T(8,128)} fusion(f32[512,8,256]{2,0,1:T(8,128)} %bitcast.30, f32[8,256,256]{2,1,0:T(8,128)S(1)} %copy-done.2, f32[8]{0:T(128)S(1)} %convert_element_type.11), kind=kOutput, calls=%fused_computation.1 | convolution fusion | flops 3221749760 | bytes 10485792 | tf_op jit(solution)/shard_map/psc,sca->psa/dot_general | solution.py:36
  194.9 5.4 %copy.62 = f32[512,8,256]{2,1,0:T(8,128)} copy(f32[512,8,256]{0,2,1:T(8,128)} %convolution_bitcast_fusion) | data formatting | bytes 8388608 | tf_op jit(solution)/shard_map/psc,sca->psa/transpose | solution.py:36
  200.3 4.3 %fusion.3 = f32[8,512,256]{2,0,1:T(8,128)S(1)} fusion(f32[512,8,256]{2,1,0:T(8,128)} %copy.62, s32[8]{0:T(128)S(1)} %get-tuple-element.5), kind=kOutput, calls=%fused_computation.13 | convolution fusion | flops 100663360 | bytes 8388640 | tf_op jit(solution)/shard_map/psa,sb->pba/dot_general | solution.py:43
  204.7 0.0 copy-start.1
  204.7 3.9 %copy.69 = f32[64,8,8,256]{3,1,2,0:T(8,128)} copy(f32[64,8,8,256]{3,2,1,0:T(8,128)S(1)} %bitcast.33) | data formatting | bytes 8388608
  208.6 0.0 reduce-scatter.2.cloned.1.call-update
  208.6 87.6 %reduce-scatter.2.cloned.1.call-done = f32[32,2048]{1,0:T(8,128)} async-done(((f32[512,2048]{1,0:T(8,128)}), f32[32,2048]{1,0:T(8,128)}) %reduce-scatter.2.cloned.1.call-update) | async-done | bytes 262160 | tf_op jit(solution)/shard_map/reduce_scatter | solution.py:50
  296.2 0.0 copy-done.1
  (6 shorter events, 0.0 us)
Async XLA Ops:
  6.5 0.7 copy-start
  55.4 7.8 %copy-start.3 = (s32[128]{0:T(128)S(1)}, s32[128]{0:T(128)}, u32[]{:S(2)}) copy-start(s32[128]{0:T(128)} %param.8) | copy-start | bytes 1540
  55.4 7.9 %copy-start.4 = (s32[128]{0:T(128)S(1)}, s32[128]{0:T(128)}, u32[]{:S(2)}) copy-start(s32[128]{0:T(128)} %param.9) | copy-start | bytes 1540
  55.4 85.3 %all-to-all-start = ((f32[16,1,65536]{2,1,0:T(1,128)}), f32[16,1,65536]{2,1,0:T(1,128)}, u32[]{:S(2)}, u32[]{:S(2)}) async-start(f32[16,1,65536]{2,1,0:T(1,128)} %reshape.71), calls=%async_computation | async-start | bytes 8388608 | tf_op jit(solution)/shard_map/all_to_all | solution.py:27
  62.9 233.2 %reduce-scatter.2.cloned.1.call-start = ((), (), s32[]{:S(2)}) async-start(), calls=%async_computation.2 | async-start | bytes 4456448 | tf_op jit(solution)/shard_map/reduce_scatter | solution.py:50
  170.4 11.6 %copy-start.2 = (f32[8,256,256]{2,1,0:T(8,128)S(1)}, f32[8,256,256]{2,1,0:T(8,128)}, u32[]{:S(2)}) copy-start(f32[8,256,256]{2,1,0:T(8,128)} %param.7) | copy-start | bytes 6291460
  204.7 91.5 %copy-start.1 = (s32[128,16]{0,1:T(8,128)S(1)}, s32[128,16]{0,1:T(8,128)}, u32[]{:S(2)}) copy-start(s32[128,16]{0,1:T(8,128)} %param.6) | copy-start | bytes 24580
Sparse Core Ops, SparseCore 0:
  208.7 87.3 reduce-scatter.1
where the time goes:
time: 304 us; the launch traced here: 303 us
  waiting for transfers between devices  165 us (54%)
  local copies, waits for them, and re-layouts  78.8 us (26%)
  other arithmetic  20.9 us (7%)
  matrix products  17.3 us (6%)
  between operations  13.5 us (4%)
  starting transfers between devices  7.79 us (3%)
    reduce_scatter x1, waiting for transfers between devices, local(): lax.psum_scatter(spread.reshape(local_rows * lax.axis_size('row'), NV), '...  87.6 us
    all_to_all x1, waiting for transfers between devices, local(): lax.all_to_all(sending, 'row', split_axis=2, concat_axis=0, tiled=True)  77.2 us
    unnamed x14, local copies, waits for them, and re-layouts  35.8 us
    gather x3, local copies, waits for them, and re-layouts, local(): picked = jnp.take(masked, wanted, axis=1)  14.3 us
    all_to_all x1, other arithmetic, local(): lax.all_to_all(sending, 'row', split_axis=2, concat_axis=0, tiled=True)  14.1 us
    dot_general x1, matrix products, local(): jnp.einsum('psc,sca->psa', columns, weights, precision=lax.Precision.HIGH...  12.9 us
    all_to_all x2, local copies, waits for them, and re-layouts, local(): lax.all_to_all(sending, 'row', split_axis=2, concat_axis=0, tiled=True)  12.1 us
    select_n x1, local copies, waits for them, and re-layouts, local(): picked = jnp.take(masked, wanted, axis=1)  10.8 us
  transfers between devices with their start and end apart: 2, of which 2 were waited for; matrix products, arithmetic and copies ran while one was open for 0% of the time, Pallas kernels for 0%

commit v1 on v0

v1 whole, which is shorter than its diff:
```python
import functools

import jax
import jax.numpy as jnp
from jax import lax
from jax.experimental import pallas as pl
from jax.experimental.pallas import tpu as pltpu
from jax.sharding import PartitionSpec as P

PTILE = 4
MESH = pl.DeviceIdType.MESH
F32 = jnp.float32
BF16 = jnp.bfloat16


def kernel(
    n, snake, nt, amps, amp_mask, integ, meta, out,
    ag, wsib, wcat, aw, prod, part, rs, fin,
    ag_recv, ag_right, ag_left, ag_sib, rs_recv, rs_send, w_sems, fin_sems,
):
    rows, width = amps.shape
    slots, tile, _ = integ.shape
    half = tile // 2
    blocks = width // tile
    hr = rows // 2
    far = n // 2
    grp = lax.axis_index("grp")
    r = lax.axis_index("row")
    chip, core = r // 2, r % 2
    other = 1 - core

    if snake:
        z, y, length = chip // 2, chip % 2, n // 2
        pos = (1 - y) * z + y * (n - 1 - z)

        def chip_at(q):
            up = q // length
            return (1 - up) * (2 * q) + up * (2 * (n - 1 - q) + 1)
    else:
        pos = chip

        def chip_at(q):
            return q

    right = (grp, chip_at((pos + 1) % n) * 2 + core)
    left = (grp, chip_at((pos + n - 1) % n) * 2 + core)
    sib_row = chip * 2 + other
    sibling = (grp, sib_row)

    barrier = pltpu.get_barrier_semaphore()
    for who in (right, left, sibling):
        pl.semaphore_signal(barrier, inc=1, device_id=who, device_id_type=MESH)

    def mine(k, c):
        return ag.at[k, c, pl.ds(pl.multiple_of(core * hr, hr), hr), :]

    mrows = rows // PTILE
    m8 = amp_mask[pl.ds(pl.multiple_of(r * mrows, mrows), mrows), :].astype(F32)
    pick = (
        lax.broadcasted_iota(jnp.int32, (rows, mrows), 0) // PTILE
        == lax.broadcasted_iota(jnp.int32, (rows, mrows), 1)
    ).astype(F32)
    mask = jnp.dot(pick, m8, preferred_element_type=F32)
    for j in range(blocks):
        seg = amps[:, j * tile:(j + 1) * tile] * mask[:, j:j + 1]
        for c in range(2):
            ag[0, c, pl.ds(pl.multiple_of(core * hr, hr), hr), j * tile:(j + 1) * tile] = (
                seg[c * hr:(c + 1) * hr]
            )

    pl.semaphore_wait(barrier, 3)

    pending = []

    def send(src, dst, ssem, rsem, who):
        cp = pltpu.make_async_remote_copy(
            src_ref=src, dst_ref=dst, send_sem=ssem, recv_sem=rsem,
            device_id=who, device_id_type=MESH,
        )
        cp.start()
        pending.append(cp)

    def got(dst, rsem, ssem, who):
        pltpu.make_async_remote_copy(
            src_ref=dst, dst_ref=dst, send_sem=ssem, recv_sem=rsem,
            device_id=who, device_id_type=MESH,
        ).wait_recv()

    def go_right(k, c):
        send(mine(k, c), mine(k + 1, c), ag_right.at[k, c], ag_recv.at[k + 1, c, 0], right)

    def go_left(k, c):
        k0 = k if k else n
        send(mine(k, c), mine(k0 - 1, c), ag_left.at[k, c], ag_recv.at[k0 - 1, c, 0], left)

    def go_sib(k, c):
        send(mine(k, c), mine(k, c), ag_sib.at[k, c], ag_recv.at[k, c, 1], sibling)

    def from_ring(k, c):
        got(mine(k, c), ag_recv.at[k, c, 0], ag_sib.at[k, c], sibling)

    def from_sib(k, c):
        theirs = ag.at[k, c, pl.ds(pl.multiple_of(other * hr, hr), hr), :]
        got(theirs, ag_recv.at[k, c, 1], ag_sib.at[k, c], sibling)

    go_right(0, 0)
    go_left(0, 1)
    go_right(0, 1)
    go_left(0, 0)
    send(
        integ.at[:, :, pl.ds(pl.multiple_of(other * half, half), half)],
        wsib, w_sems.at[0], w_sems.at[1], sibling,
    )
    go_sib(0, 0)
    go_sib(0, 1)

    def put_w(j, w):
        hi = w.astype(BF16)
        wcat[j, :, :half] = hi
        wcat[j, :, half:] = (w - hi.astype(F32)).astype(BF16)

    @pl.loop(0, slots)
    def _(s):
        w = integ[s, :, pl.ds(pl.multiple_of(core * half, half), half)]
        put_w(s, w)

    got(wsib, w_sems.at[1], w_sems.at[0], sibling)

    @pl.loop(0, slots)
    def _(s):
        put_w(slots + s, wsib[s])

    def info(b, j):
        if j < slots:
            return meta[b, r * slots + j]
        return meta[b, sib_row * slots + j - slots]

    def compute(k):
        @pl.loop(0, blocks)
        def _(q):
            cols = pl.ds(pl.multiple_of(q * tile, tile), tile)
            for c in range(2):
                x = ag[k, c, :, cols]
                hi = x.astype(BF16)
                aw[q, c * rows:(c + 1) * rows, :] = hi
                aw[q, (2 + c) * rows:(3 + c) * rows, :] = (x - hi.astype(F32)).astype(BF16)

        for j in range(2 * slots):
            d = jnp.dot(aw[info(nt, j)], wcat[j], preferred_element_type=F32)
            top, low = d[:2 * rows], d[2 * rows:]
            prod[j] = (low[:, half:] + low[:, :half]) + top[:, half:] + top[:, :half]

        for b in range(nt):
            acc = None
            for j in range(2 * slots):
                term = prod[j] * info(b, j).astype(F32)
                acc = term if acc is None else acc + term
            for c in range(2):
                part[k, c, :, b * half:(b + 1) * half] = acc[c * rows:(c + 1) * rows]

    from_sib(0, 0)
    from_sib(0, 1)
    compute(0)

    for h in range(1, far):
        for c in range(2):
            cr, cl = c, 1 - c
            from_ring(h, cr)
            if h < far - 1 or cr == 0:
                go_right(h, cr)
            from_ring(n - h, cl)
            if h < far - 1 or cl == 1:
                go_left(n - h, cl)
            go_sib(h, cr)
            go_sib(n - h, cl)
        for k in (h, n - h):
            from_sib(k, 0)
            from_sib(k, 1)
            compute(k)

    def sum_right(k, c):
        send(part.at[k, c], rs.at[k + 1, c], rs_send.at[k, c, 0], rs_recv.at[k + 1, c], right)

    def sum_left(k, c):
        send(part.at[k, c], rs.at[k - 1, c], rs_send.at[k, c, 1], rs_recv.at[k - 1, c], left)

    def sum_got(k, c):
        got(rs.at[k, c], rs_recv.at[k, c], rs_send.at[k % n, c, 0], right)

    sum_right(far + 1, 1)
    sum_left(far - 1, 0)
    from_ring(far, 0)
    go_sib(far, 0)
    from_ring(far, 1)
    go_sib(far, 1)
    from_sib(far, 0)
    from_sib(far, 1)
    compute(far)
    sum_right(far, 0)
    sum_left(far, 1)

    def relay(k, c, onward):
        sum_got(k, c)
        if 0 < k < n:
            part[k, c] = part[k, c] + rs[k, c]
            onward(k, c)

    for t in range(1, far + 1):
        if far + 1 + t <= n:
            relay(far + 1 + t, 1, sum_right)
            relay(far - 1 - t, 0, sum_left)
        relay(far + t, 0, sum_right)
        relay(far - t, 1, sum_left)

    for c in range(2):
        part[0, c] = part[0, c] + rs[0, c] + rs[n, c]
    for c in range(2):
        send(
            part.at[0, c, pl.ds(pl.multiple_of(other * hr, hr), hr), :],
            fin.at[c], fin_sems.at[0, c], fin_sems.at[1, c], sibling,
        )
    for c in range(2):
        for b in range(nt):
            out[c * hr:(c + 1) * hr, pl.ds(pl.multiple_of(b * tile + core * half, half), half)] = (
                part[0, c, pl.ds(pl.multiple_of(core * hr, hr), hr), b * half:(b + 1) * half]
            )
    for c in range(2):
        got(fin.at[c], fin_sems.at[1, c], fin_sems.at[0, c], sibling)
        for b in range(nt):
            out[c * hr:(c + 1) * hr, pl.ds(pl.multiple_of(b * tile + other * half, half), half)] = (
                fin[c, :, b * half:(b + 1) * half]
            )
    for cp in pending:
        cp.wait_send()


def local(members, amps, amp_mask, integrals, slot_tile, int_mask):
    rows, width = amps.shape
    slots, tile, _ = integrals.shape
    nt = slot_tile.shape[0] // (width // tile)
    n = members // 2
    hr, half = rows // 2, tile // 2
    ids = jnp.arange(slot_tile.shape[0], dtype=jnp.int32)
    on = jnp.sum(jnp.where(slot_tile[None, :] == ids[:, None], int_mask[:, None], 0), axis=0)
    line = jnp.arange(nt + 1, dtype=jnp.int32)[:, None]
    meta = jnp.where(
        line < nt, jnp.where(slot_tile[None, :] % nt == line, on[None, :], 0), slot_tile[None, :] // nt
    )
    vmem = pl.BlockSpec(memory_space=pltpu.VMEM)
    smem = pl.BlockSpec(memory_space=pltpu.SMEM)
    dma = pltpu.SemaphoreType.DMA
    return pl.pallas_call(
        functools.partial(kernel, n, n == 8, nt),
        out_shape=jax.ShapeDtypeStruct((rows, nt * tile), F32),
        in_specs=[vmem, vmem, vmem, smem],
        out_specs=vmem,
        scratch_shapes=[
            pltpu.VMEM((n, 2, rows, width), F32),
            pltpu.VMEM((slots, tile, half), F32),
            pltpu.VMEM((2 * slots, tile, tile), BF16),
            pltpu.VMEM((width // tile, 4 * rows, tile), BF16),
            pltpu.VMEM((2 * slots, 2 * rows, half), F32),
            pltpu.VMEM((n, 2, rows, nt * half), F32),
            pltpu.VMEM((n + 1, 2, rows, nt * half), F32),
            pltpu.VMEM((2, hr, nt * half), F32),
            dma((n, 2, 2)),
            dma((n, 2)),
            dma((n, 2)),
            dma((n, 2)),
            dma((n + 1, 2)),
            dma((n, 2, 2)),
            dma((2,)),
            dma((2, 2)),
        ],
        compiler_params=pltpu.CompilerParams(
            collective_id=0, has_side_effects=True, vmem_limit_bytes=60 * 1024 * 1024
        ),
        cost_estimate=pl.CostEstimate(
            flops=8 * n * 2 * rows * slots * tile * tile,
            bytes_accessed=4 * (rows * width + slots * tile * tile + rows * nt * tile),
            transcendentals=0,
        ),
    )(amps, amp_mask, integrals, meta)


def solution(mesh):
    return jax.shard_map(
        functools.partial(local, mesh.shape["row"]),
        mesh=mesh,
        in_specs=(
            P(("grp", "row"), None),
            P("grp", None),
            P(("grp", "row"), None, None),
            P("grp"),
            P("grp"),
        ),
        out_specs=P(("grp", "row"), None),
        check_vma=False,
    )
```

time: 304 us -> 78.1 us (0.26)
  waiting for transfers between devices: 165 us -> 0 us
  local copies, waits for them, and re-layouts: 78.8 us -> 3.1 us
  Pallas kernels: 0 us -> 72.7 us
  other arithmetic: 20.9 us -> 2.1 us
  matrix products: 17.3 us -> 0 us
  between operations: 13.5 us -> 0.02 us
  starting transfers between devices: 7.79 us -> 0 us
    reduce_scatter x1 -> x0, waiting for transfers between devices: 87.6 us -> none  [local(): lax.psum_scatter(spread.reshape(local_rows * lax.axis_size('row'), NV), '...]
    all_to_all x1 -> x0, waiting for transfers between devices: 77.2 us -> none  [local(): lax.all_to_all(sending, 'row', split_axis=2, concat_axis=0, tiled=True)]
    pallas_call x0 -> x1, Pallas kernels: none -> 72.7 us  [local(): pl.pallas_call(functools.partial(kernel, n, n == 8, nt), out_shape=jax.Sh...]
    unnamed x14 -> x2, local copies, waits for them, and re-layouts: 35.8 us -> 3.1 us
    dot_general x2 -> x0, matrix products: 17.3 us -> none  [the longest x1 12.9 us: local(): jnp.einsum('psc,sca->psa', columns, weights, precision=lax.Precision.HIGH...]
    gather x3 -> x0, local copies, waits for them, and re-layouts: 14.3 us -> none  [local(): picked = jnp.take(masked, wanted, axis=1)]
    all_to_all x1 -> x0, other arithmetic: 14.1 us -> none  [local(): lax.all_to_all(sending, 'row', split_axis=2, concat_axis=0, tiled=True)]
    all_to_all x2 -> x0, local copies, waits for them, and re-layouts: 12.1 us -> none  [local(): lax.all_to_all(sending, 'row', split_axis=2, concat_axis=0, tiled=True)]
  transfers between devices with their start and end apart: 2 -> 0, of which waited for: 2 -> 0; matrix products, arithmetic and copies ran while one was open for 0% -> 0% of each run, Pallas kernels for 0% -> 0%
where the time goes in v1:
time: 78.1 us; the launch traced here: 77.9 us
  Pallas kernels  72.7 us (93%)
  local copies, waits for them, and re-layouts  3.1 us (4%)
  other arithmetic  2.1 us (3%)
    pallas_call x1, Pallas kernels, local(): pl.pallas_call(functools.partial(kernel, n, n == 8, nt), out_shape=jax.Sh...  72.7 us
    unnamed x2, local copies, waits for them, and re-layouts  3.1 us

profile of v1, /device:TPU:0, one launch (start us, length us, event | category | flops | bytes accessed | tf_op | source)
XLA Modules:
  0.0 77.9 jit_solution(11232782730716401385)
XLA Ops:
  0.0 0.8 select_reduce_fusion
  0.8 0.7 and_select_fusion.1
  1.4 0.7 select_select_fusion.meta
  2.1 1.4 %copy.7.amp_mask = s32[128,16]{1,0:T(8,128)} copy(s32[128,16]{0,1:T(8,128)} %param.6) | data formatting | bytes 16384 | tf_op args[1]
  3.5 72.7 %shard_map.55 = f32[32,2048]{1,0:T(8,128)} custom-call(f32[32,4096]{1,0:T(8,128)} %amps.1, s32[128,16]{1,0:T(8,128)} %copy.7.amp_mask, f32[8,256,256]{2,1,0:T(8,128)} %integ.1, s32[9,128]{1,0:T(8,128)} %select_select_fusion.meta), custom_call_target="tpu_custom_call" | custom-call | flops 2147483648 | bytes 2883584 | tf_op jit(solution)/shard_map/pallas_call | solution.py:252
  76.2 1.7 %copy.9 = f32[32,2048]{1,0:T(8,128)} copy(f32[32,2048]{1,0:T(8,128)} %shard_map.55) | data formatting | bytes 524288
  (1 shorter events, 0.0 us)

commit v2 on v1

--- a/solution.py
+++ b/solution.py
@@ -14,9 +14,9 @@
 
 
 def kernel(
-    n, snake, nt, amps, amp_mask, integ, meta, out,
-    ag, wsib, wcat, aw, prod, part, rs, fin,
-    ag_recv, ag_right, ag_left, ag_sib, rs_recv, rs_send, w_sems, fin_sems,
+    n, snake, nt, amps, mask_t, integ, slot_tile, int_mask, out,
+    ag, wown, wsib, gain_v, gain, block_v, block, wcat, aw, prod, part, rs, fin,
+    ag_recv, ag_right, ag_left, ag_sib, rs_recv, rs_send, w_sems, fin_sems, own_sems,
 ):
     rows, width = amps.shape
     slots, tile, _ = integ.shape
@@ -54,13 +54,20 @@
     def mine(k, c):
         return ag.at[k, c, pl.ds(pl.multiple_of(core * hr, hr), hr), :]
 
-    mrows = rows // PTILE
-    m8 = amp_mask[pl.ds(pl.multiple_of(r * mrows, mrows), mrows), :].astype(F32)
+    own_w = pltpu.make_async_copy(
+        integ.at[:, :, pl.ds(pl.multiple_of(core * half, half), half)], wown, own_sems.at[0]
+    )
+    own_w.start()
+
+    mrows = mask_t.shape[1]
+    shape = (rows, mrows)
     pick = (
-        lax.broadcasted_iota(jnp.int32, (rows, mrows), 0) // PTILE
-        == lax.broadcasted_iota(jnp.int32, (rows, mrows), 1)
+        lax.broadcasted_iota(jnp.int32, shape, 1)
+        == lax.broadcasted_iota(jnp.int32, shape, 0) // PTILE + r * (rows // PTILE)
     ).astype(F32)
-    mask = jnp.dot(pick, m8, preferred_element_type=F32)
+    mask = lax.dot_general(
+        pick, mask_t[...].astype(F32), (((1,), (1,)), ((), ())), preferred_element_type=F32
+    )
     for j in range(blocks):
         seg = amps[:, j * tile:(j + 1) * tile] * mask[:, j:j + 1]
         for c in range(2):
@@ -114,15 +121,31 @@
     go_sib(0, 0)
     go_sib(0, 1)
 
+    count = slot_tile.shape[1]
+    tiles = jnp.broadcast_to(slot_tile[...], (count, count))
+    hot = (tiles == lax.broadcasted_iota(jnp.int32, (count, count), 0)).astype(F32)
+    on = jnp.dot(int_mask[...].astype(F32), hot, preferred_element_type=F32)
+    tiles = jnp.broadcast_to(slot_tile[...], (nt, count))
+    here = (tiles % nt == lax.broadcasted_iota(jnp.int32, (nt, count), 0)).astype(F32)
+    gain_v[...] = here * on
+    block_v[...] = tiles // nt
+    tables = (
+        pltpu.make_async_copy(gain_v, gain, own_sems.at[1]),
+        pltpu.make_async_copy(block_v, block, own_sems.at[2]),
+    )
+    for cp in tables:
+        cp.start()
+
     def put_w(j, w):
         hi = w.astype(BF16)
         wcat[j, :, :half] = hi
         wcat[j, :, half:] = (w - hi.astype(F32)).astype(BF16)
 
+    own_w.wait()
+
     @pl.loop(0, slots)
     def _(s):
-        w = integ[s, :, pl.ds(pl.multiple_of(core * half, half), half)]
-        put_w(s, w)
+        put_w(s, wown[s])
 
     got(wsib, w_sems.at[1], w_sems.at[0], sibling)
 
@@ -130,10 +153,11 @@
     def _(s):
         put_w(slots + s, wsib[s])
 
-    def info(b, j):
-        if j < slots:
-            return meta[b, r * slots + j]
-        return meta[b, sib_row * slots + j - slots]
+    for cp in tables:
+        cp.wait()
+
+    def slot_of(j):
+        return r * slots + j if j < slots else sib_row * slots + j - slots
 
     def compute(k):
         @pl.loop(0, blocks)
@@ -146,14 +170,14 @@
                 aw[q, (2 + c) * rows:(3 + c) * rows, :] = (x - hi.astype(F32)).astype(BF16)
 
         for j in range(2 * slots):
-            d = jnp.dot(aw[info(nt, j)], wcat[j], preferred_element_type=F32)
+            d = jnp.dot(aw[block[0, slot_of(j)]], wcat[j], preferred_element_type=F32)
             top, low = d[:2 * rows], d[2 * rows:]
             prod[j] = (low[:, half:] + low[:, :half]) + top[:, half:] + top[:, :half]
 
         for b in range(nt):
             acc = None
             for j in range(2 * slots):
-                term = prod[j] * info(b, j).astype(F32)
+                term = prod[j] * gain[b, slot_of(j)]
                 acc = term if acc is None else acc + term
             for c in range(2):
                 part[k, c, :, b * half:(b + 1) * half] = acc[c * rows:(c + 1) * rows]
@@ -240,23 +264,22 @@
     nt = slot_tile.shape[0] // (width // tile)
     n = members // 2
     hr, half = rows // 2, tile // 2
-    ids = jnp.arange(slot_tile.shape[0], dtype=jnp.int32)
-    on = jnp.sum(jnp.where(slot_tile[None, :] == ids[:, None], int_mask[:, None], 0), axis=0)
-    line = jnp.arange(nt + 1, dtype=jnp.int32)[:, None]
-    meta = jnp.where(
-        line < nt, jnp.where(slot_tile[None, :] % nt == line, on[None, :], 0), slot_tile[None, :] // nt
-    )
     vmem = pl.BlockSpec(memory_space=pltpu.VMEM)
-    smem = pl.BlockSpec(memory_space=pltpu.SMEM)
+    count = slot_tile.shape[0]
     dma = pltpu.SemaphoreType.DMA
     return pl.pallas_call(
         functools.partial(kernel, n, n == 8, nt),
         out_shape=jax.ShapeDtypeStruct((rows, nt * tile), F32),
-        in_specs=[vmem, vmem, vmem, smem],
+        in_specs=[vmem, vmem, pl.BlockSpec(memory_space=pl.ANY), vmem, vmem],
         out_specs=vmem,
         scratch_shapes=[
             pltpu.VMEM((n, 2, rows, width), F32),
             pltpu.VMEM((slots, tile, half), F32),
+            pltpu.VMEM((slots, tile, half), F32),
+            pltpu.VMEM((nt, count), F32),
+            pltpu.SMEM((nt, count), F32),
+            pltpu.VMEM((nt, count), jnp.int32),
+            pltpu.SMEM((nt, count), jnp.int32),
             pltpu.VMEM((2 * slots, tile, tile), BF16),
             pltpu.VMEM((width // tile, 4 * rows, tile), BF16),
             pltpu.VMEM((2 * slots, 2 * rows, half), F32),
@@ -271,6 +294,7 @@
             dma((n, 2, 2)),
             dma((2,)),
             dma((2, 2)),
+            dma((3,)),
         ],
         compiler_params=pltpu.CompilerParams(
             collective_id=0, has_side_effects=True, vmem_limit_bytes=60 * 1024 * 1024
@@ -280,7 +304,7 @@
             bytes_accessed=4 * (rows * width + slots * tile * tile + rows * nt * tile),
             transcendentals=0,
         ),
-    )(amps, amp_mask, integrals, meta)
+    )(amps, amp_mask.T, integrals, slot_tile.reshape(1, count), int_mask.reshape(1, count))
 
 
 def solution(mesh):

time: 78.1 us -> 73.8 us (0.945)
  other arithmetic: 2.1 us -> 0 us
  local copies, waits for them, and re-layouts: 3.1 us -> 1.67 us
    unnamed x2 -> x1, local copies, waits for them, and re-layouts: 3.1 us -> 1.67 us
    select_n x2 -> x0, other arithmetic: 1.33 us -> none  [the longest x1 0.67 us: local(): slot_tile[None, :] % nt == line]
where the time goes in v2:
time: 73.8 us; the launch traced here: 73.7 us
  Pallas kernels  72 us (98%)
  local copies, waits for them, and re-layouts  1.67 us (2%)
    pallas_call x1, Pallas kernels, local(): pl.pallas_call(functools.partial(kernel, n, n == 8, nt), out_shape=jax.Sh...  72 us
    unnamed x1, local copies, waits for them, and re-layouts  1.67 us

profile of v2, /device:TPU:0, one launch (start us, length us, event | category | flops | bytes accessed | tf_op | source)
XLA Modules:
  0.0 73.7 jit_solution(6370115335682190020)
XLA Ops:
  0.0 72.0 %shard_map.55 = f32[32,2048]{1,0:T(8,128)} custom-call(f32[32,4096]{1,0:T(8,128)} %amps.1, s32[16,128]{1,0:T(8,128)} %bitcast.3, f32[8,256,256]{2,1,0:T(8,128)} %integ.1, s32[1,128]{1,0:T(1,128)} %bitcast.4, s32[1,128]{1,0:T(1,128)} %bitcast.5), custom_call_target="tpu_custom_call" | custom-call | flops 2147483648 | bytes 2883584 | tf_op jit(solution)/shard_map/pallas_call | solution.py:270
  72.0 1.7 %copy.7 = f32[32,2048]{1,0:T(8,128)} copy(f32[32,2048]{1,0:T(8,128)} %shard_map.55) | data formatting | bytes 524288

commit v3 on v2

--- a/solution.py
+++ b/solution.py
@@ -15,8 +15,8 @@
 
 def kernel(
     n, snake, nt, amps, mask_t, integ, slot_tile, int_mask, out,
-    ag, wown, wsib, gain_v, gain, block_v, block, wcat, aw, prod, part, rs, fin,
-    ag_recv, ag_right, ag_left, ag_sib, rs_recv, rs_send, w_sems, fin_sems, own_sems,
+    ag, wown, wsib, gain_v, gain, block_v, block, wcat, aw, prod, part, rs, last, fin,
+    ag_recv, ag_right, ag_left, ag_sib, rs_recv, rs_send, w_sems, fin_sems, own_sems, last_recv, last_send,
 ):
     rows, width = amps.shape
     slots, tile, _ = integ.shape
@@ -42,13 +42,14 @@
         def chip_at(q):
             return q
 
-    right = (grp, chip_at((pos + 1) % n) * 2 + core)
-    left = (grp, chip_at((pos + n - 1) % n) * 2 + core)
+    right_chip, left_chip = chip_at((pos + 1) % n), chip_at((pos + n - 1) % n)
+    right, right_other = (grp, right_chip * 2 + core), (grp, right_chip * 2 + other)
+    left, left_other = (grp, left_chip * 2 + core), (grp, left_chip * 2 + other)
     sib_row = chip * 2 + other
     sibling = (grp, sib_row)
 
     barrier = pltpu.get_barrier_semaphore()
-    for who in (right, left, sibling):
+    for who in (right, left, right_other, left_other, sibling):
         pl.semaphore_signal(barrier, inc=1, device_id=who, device_id_type=MESH)
 
     def mine(k, c):
@@ -75,7 +76,7 @@
                 seg[c * hr:(c + 1) * hr]
             )
 
-    pl.semaphore_wait(barrier, 3)
+    pl.semaphore_wait(barrier, 5)
 
     pending = []
 
@@ -107,8 +108,8 @@
         got(mine(k, c), ag_recv.at[k, c, 0], ag_sib.at[k, c], sibling)
 
     def from_sib(k, c):
-        theirs = ag.at[k, c, pl.ds(pl.multiple_of(other * hr, hr), hr), :]
-        got(theirs, ag_recv.at[k, c, 1], ag_sib.at[k, c], sibling)
+        rest = ag.at[k, c, pl.ds(pl.multiple_of(other * hr, hr), hr), :]
+        got(rest, ag_recv.at[k, c, 1], ag_sib.at[k, c], sibling)
 
     go_right(0, 0)
     go_left(0, 1)
@@ -185,6 +186,12 @@
     from_sib(0, 0)
     from_sib(0, 1)
     compute(0)
+    own = pl.ds(pl.multiple_of(core * hr, hr), hr)
+    theirs = pl.ds(pl.multiple_of(other * hr, hr), hr)
+    for c in range(2):
+        send(
+            part.at[0, c, theirs, :], fin.at[c], fin_sems.at[0, c], fin_sems.at[1, c], sibling
+        )
 
     for h in range(1, far):
         for c in range(2):
@@ -202,14 +209,25 @@
             from_sib(k, 1)
             compute(k)
 
+    def deliver(k, c, way, same, cross):
+        send(
+            part.at[k, c, own, :], last.at[way, c, core],
+            rs_send.at[k, c, way], last_recv.at[way, c, core], same,
+        )
+        send(
+            part.at[k, c, theirs, :], last.at[way, c, core],
+            last_send.at[way, c], last_recv.at[way, c, core], cross,
+        )
+
     def sum_right(k, c):
+        if k + 1 == n:
+            return deliver(k, c, 0, right, right_other)
         send(part.at[k, c], rs.at[k + 1, c], rs_send.at[k, c, 0], rs_recv.at[k + 1, c], right)
 
     def sum_left(k, c):
+        if k == 1:
+            return deliver(k, c, 1, left, left_other)
         send(part.at[k, c], rs.at[k - 1, c], rs_send.at[k, c, 1], rs_recv.at[k - 1, c], left)
-
-    def sum_got(k, c):
-        got(rs.at[k, c], rs_recv.at[k, c], rs_send.at[k % n, c, 0], right)
 
     sum_right(far + 1, 1)
     sum_left(far - 1, 0)
@@ -217,43 +235,36 @@
     go_sib(far, 0)
     from_ring(far, 1)
     go_sib(far, 1)
+
+    def relay(k, c, onward):
+        if 0 < k < n:
+            got(rs.at[k, c], rs_recv.at[k, c], rs_send.at[k, c, 0], right)
+            part[k, c] = part[k, c] + rs[k, c]
+            onward(k, c)
+
     from_sib(far, 0)
     from_sib(far, 1)
     compute(far)
     sum_right(far, 0)
     sum_left(far, 1)
-
-    def relay(k, c, onward):
-        sum_got(k, c)
-        if 0 < k < n:
-            part[k, c] = part[k, c] + rs[k, c]
-            onward(k, c)
-
-    for t in range(1, far + 1):
-        if far + 1 + t <= n:
-            relay(far + 1 + t, 1, sum_right)
-            relay(far - 1 - t, 0, sum_left)
+    for t in range(1, far):
+        relay(far + 1 + t, 1, sum_right)
+        relay(far - 1 - t, 0, sum_left)
         relay(far + t, 0, sum_right)
         relay(far - t, 1, sum_left)
 
     for c in range(2):
-        part[0, c] = part[0, c] + rs[0, c] + rs[n, c]
+        got(fin.at[c], fin_sems.at[1, c], fin_sems.at[0, c], sibling)
     for c in range(2):
-        send(
-            part.at[0, c, pl.ds(pl.multiple_of(other * hr, hr), hr), :],
-            fin.at[c], fin_sems.at[0, c], fin_sems.at[1, c], sibling,
-        )
-    for c in range(2):
-        for b in range(nt):
-            out[c * hr:(c + 1) * hr, pl.ds(pl.multiple_of(b * tile + core * half, half), half)] = (
-                part[0, c, pl.ds(pl.multiple_of(core * hr, hr), hr), b * half:(b + 1) * half]
-            )
-    for c in range(2):
-        got(fin.at[c], fin_sems.at[1, c], fin_sems.at[0, c], sibling)
-        for b in range(nt):
-            out[c * hr:(c + 1) * hr, pl.ds(pl.multiple_of(b * tile + other * half, half), half)] = (
-                fin[c, :, b * half:(b + 1) * half]
-            )
+        for way in ((0, 1) if c else (1, 0)):
+            for q in range(2):
+                got(last.at[way, c, q], last_recv.at[way, c, q], last_send.at[way, c], right)
+        for src, q in ((part.at[0, c, own, :], core), (fin.at[c], other)):
+            for b in range(nt):
+                cols = slice(b * half, (b + 1) * half)
+                out[c * hr:(c + 1) * hr, pl.ds(pl.multiple_of(b * tile + q * half, half), half)] = (
+                    src[:, cols] + last[0, c, q, :, cols] + last[1, c, q, :, cols]
+                )
     for cp in pending:
         cp.wait_send()
 
@@ -284,17 +295,20 @@
             pltpu.VMEM((width // tile, 4 * rows, tile), BF16),
             pltpu.VMEM((2 * slots, 2 * rows, half), F32),
             pltpu.VMEM((n, 2, rows, nt * half), F32),
-            pltpu.VMEM((n + 1, 2, rows, nt * half), F32),
+            pltpu.VMEM((n, 2, rows, nt * half), F32),
+            pltpu.VMEM((2, 2, 2, hr, nt * half), F32),
             pltpu.VMEM((2, hr, nt * half), F32),
             dma((n, 2, 2)),
             dma((n, 2)),
             dma((n, 2)),
             dma((n, 2)),
-            dma((n + 1, 2)),
+            dma((n, 2)),
             dma((n, 2, 2)),
             dma((2,)),
             dma((2, 2)),
             dma((3,)),
+            dma((2, 2, 2)),
+            dma((2, 2)),
         ],
         compiler_params=pltpu.CompilerParams(
             collective_id=0, has_side_effects=True, vmem_limit_bytes=60 * 1024 * 1024

time: 73.8 us -> 73.7 us (level)
  no operation moved by 1% of the time
where the time goes in v3:
time: 73.7 us; the launch traced here: 73.6 us
  Pallas kernels  71.9 us (98%)
  local copies, waits for them, and re-layouts  1.67 us (2%)
    pallas_call x1, Pallas kernels, local(): pl.pallas_call(functools.partial(kernel, n, n == 8, nt), out_shape=jax.Sh...  71.9 us
    unnamed x1, local copies, waits for them, and re-layouts  1.67 us

profile of v3, /device:TPU:0, one launch (start us, length us, event | category | flops | bytes accessed | tf_op | source)
XLA Modules:
  0.0 73.6 jit_solution(8159799430839323539)
XLA Ops:
  0.0 71.9 %shard_map.55 = f32[32,2048]{1,0:T(8,128)} custom-call(f32[32,4096]{1,0:T(8,128)} %amps.1, s32[16,128]{1,0:T(8,128)} %bitcast.3, f32[8,256,256]{2,1,0:T(8,128)} %integ.1, s32[1,128]{1,0:T(1,128)} %bitcast.4, s32[1,128]{1,0:T(1,128)} %bitcast.5), custom_call_target="tpu_custom_call" | custom-call | flops 2147483648 | bytes 2883584 | tf_op jit(solution)/shard_map/pallas_call | solution.py:281
  71.9 1.7 %copy.7 = f32[32,2048]{1,0:T(8,128)} copy(f32[32,2048]{1,0:T(8,128)} %shard_map.55) | data formatting | bytes 524288

commit v4 on v3

--- a/solution.py
+++ b/solution.py
@@ -242,14 +242,16 @@
             part[k, c] = part[k, c] + rs[k, c]
             onward(k, c)
 
+    relay(far + 2, 1, sum_right)
+    relay(far - 2, 0, sum_left)
     from_sib(far, 0)
     from_sib(far, 1)
     compute(far)
     sum_right(far, 0)
     sum_left(far, 1)
     for t in range(1, far):
-        relay(far + 1 + t, 1, sum_right)
-        relay(far - 1 - t, 0, sum_left)
+        relay(far + 2 + t, 1, sum_right)
+        relay(far - 2 - t, 0, sum_left)
         relay(far + t, 0, sum_right)
         relay(far - t, 1, sum_left)
 

time: 73.7 us -> 73.6 us (level)
  no operation moved by 1% of the time
where the time goes in v4:
time: 73.6 us; the launch traced here: 73.4 us
  Pallas kernels  71.7 us (97%)
  local copies, waits for them, and re-layouts  1.67 us (2%)
    pallas_call x1, Pallas kernels, local(): pl.pallas_call(functools.partial(kernel, n, n == 8, nt), out_shape=jax.Sh...  71.7 us
    unnamed x1, local copies, waits for them, and re-layouts  1.67 us

profile of v4, /device:TPU:0, one launch (start us, length us, event | category | flops | bytes accessed | tf_op | source)
XLA Modules:
  0.0 73.4 jit_solution(11399595562815253617)
XLA Ops:
  0.0 71.7 %shard_map.55 = f32[32,2048]{1,0:T(8,128)} custom-call(f32[32,4096]{1,0:T(8,128)} %amps.1, s32[16,128]{1,0:T(8,128)} %bitcast.3, f32[8,256,256]{2,1,0:T(8,128)} %integ.1, s32[1,128]{1,0:T(1,128)} %bitcast.4, s32[1,128]{1,0:T(1,128)} %bitcast.5), custom_call_target="tpu_custom_call" | custom-call | flops 2147483648 | bytes 2883584 | tf_op jit(solution)/shard_map/pallas_call | solution.py:283
  71.7 1.7 %copy.7 = f32[32,2048]{1,0:T(8,128)} copy(f32[32,2048]{1,0:T(8,128)} %shard_map.55) | data formatting | bytes 524288
